TPU v7x, 512 devices: a whole 4x4x16 slice. The times are simulated.
512 devices in a mesh: inp: 64 (over z, y_hi, core), tm: 8 (over x, y_lo).
Axes of the slice: x: 4, y: 4 (y_hi: 2, y_lo: 2; y = y_hi * 2 + y_lo), z: 16, core: 2. Of those that a mesh axis runs over, the one named last changes fastest.
Arguments:
- samples: bfloat16 [512, 262144], P('inp', 'tm'), may hold values from -6 to 6
- gains: float32 [2, 256, 512], P(None, None, 'inp'), may hold values from -4 to 4
Outputs:
- spectra: bfloat16 [2, 256, 512, 128], P(None, None, 'inp', 'tm')
- visibilities: float32 [512, 256, 512], P('tm', 'inp')
All inputs are finite; a program needn't handle non-finite values.
Results may differ from a plain program's by a relative error of at most 0.0057.
Values may be sent and summed in bfloat16 or wider, within the bound.
No kernel may reach another device: no remote copies, remote signals or barrier semaphores. Data moves between devices by JAX's collectives and lax.ppermute only.
A program may use at most 64 MiB of HBM per device.

v0:
```python
import math

import jax
import jax.numpy as jnp
import numpy as np
from jax import lax
from jax.experimental import pallas as pl
from jax.experimental.pallas import tpu as pltpu
from jax.sharding import Mesh, PartitionSpec as P

NFFT = 2048
CH = 256
FIRST = 384
TAPS = 4
NEAR = 4
EARLY = 4
STEP = 256
LANES = 128
VMEM = pl.BlockSpec(memory_space=pltpu.VMEM)
ANY = pl.BlockSpec(memory_space=pl.ANY)
SMEM = pl.BlockSpec(memory_space=pltpu.SMEM)
OWN_PART_VMEM = 59 * 1024 * 1024 + 768 * 1024
PARAMS = pltpu.CompilerParams(vmem_limit_bytes=32 * 1024 * 1024)


def filter_window():
    length = TAPS * NFFT
    position = np.arange(length, dtype=np.float64)
    centred = (position - 0.5 * length + 0.5) / NFFT
    hann_taper = 0.5 - 0.5 * np.cos(2.0 * math.pi * (position + 0.5) / length)
    return np.sinc(centred) * hann_taper


def build_table(window):
    norm_scale = 1.0 / np.sqrt(np.sum(window * window))
    sample = np.arange(NFFT)[:, None]
    channel = FIRST + np.arange(CH)[None, :]
    phase_angle = 2.0 * math.pi / NFFT * (sample * channel % NFFT)
    cosine = np.cos(phase_angle) * norm_scale
    sine = -np.sin(phase_angle) * norm_scale
    return np.concatenate([cosine, sine], axis=1).astype(jnp.bfloat16)


def tapped_block(samples_ref, window_ref, frames_sent, block):
    inputs_here, count = samples_ref.shape
    frames_here = count // NFFT
    low = block * STEP
    sums = []
    for frame in range(frames_sent):
        total = jnp.zeros((inputs_here, STEP), jnp.float32)
        for tap in range(TAPS):
            source = frame - TAPS + 1 + tap
            if 0 <= source < frames_here:
                start = source * NFFT + low
                values = samples_ref[:, start : start + STEP]
                weights = window_ref[tap : tap + 1, low : low + STEP]
                total = total + weights * values.astype(jnp.float32)
        sums.append(total)
    pairs = [
        jnp.concatenate(sums[frame : frame + 2], axis=0).astype(jnp.bfloat16)
        for frame in range(0, frames_sent, 2)
    ]
    return jnp.concatenate(pairs, axis=0)


def turn_granules(blocks, size):
    count = len(blocks)
    lanes = count * size
    granule = lax.broadcasted_iota(jnp.int32, blocks[0].shape, 1) // size
    blocks = list(blocks)
    distance = count // 2
    while distance:
        upper = (granule & distance) != 0
        shift = distance * size
        for index in range(count):
            if index & distance:
                continue
            low, high = blocks[index], blocks[index + distance]
            blocks[index] = jnp.where(upper, pltpu.roll(high, shift, 1), low)
            blocks[index + distance] = jnp.where(upper, high, pltpu.roll(low, lanes - shift, 1))
        distance //= 2
    return blocks


def place_in_column(place, far):
    return (place + far * 3 // 8) % far


def own_part_kernel(
    far,
    samples_hbm,
    window_hbm,
    twiddle_hbm,
    gains_hbm,
    own_hbm,
    passed_hbm,
    parcels_hbm,
    samples_ref,
    window_ref,
    twiddle_ref,
    gains_ref,
    direct_ref,
    parcels_ref,
    arrived,
    left,
):
    inputs_here = gains_ref.shape[1]
    frames_here = samples_hbm.shape[1] // NFFT
    blocks = range(NFFT // STEP)
    fetches = []

    def fetch(source, target):
        fetches.append(pltpu.make_async_copy(source, target, arrived.at[len(fetches)]))
        fetches[-1].start()
        return fetches[-1]

    samples_in = fetch(samples_hbm, samples_ref)
    window_in = fetch(window_hbm, window_ref)
    table_in = []
    for block in blocks[: len(blocks) // 2]:
        rows = pl.ds(block * STEP, STEP)
        table_in.append(fetch(twiddle_hbm.at[rows, :], twiddle_ref.at[rows, :]))
    gains_in = fetch(gains_hbm, gains_ref)
    samples_in.wait()
    window_in.wait()
    total = None
    sent = frames_here + EARLY
    for block, table in enumerate(table_in):
        tapped = [
            tapped_block(samples_ref, window_ref, sent, half + block)
            for half in (0, len(table_in))
        ]
        table.wait()
        product = jnp.dot(
            jnp.concatenate(tapped, axis=0),
            twiddle_ref[block * STEP : (block + 1) * STEP, :],
            preferred_element_type=jnp.float32,
        )
        total = product if total is None else total + product
    channel = FIRST + lax.broadcasted_iota(jnp.int32, (1, 2 * CH), 1)
    sign = (1 - 2 * (channel % 2)).astype(jnp.float32)
    direct_ref[...] = total[: sent * inputs_here] + sign * total[sent * inputs_here :]
    own_rows = own_hbm.shape[0]
    passed_rows = passed_hbm.shape[0]
    stores = [
        pltpu.make_async_copy(direct_ref.at[pl.ds(0, own_rows), :], own_hbm, left.at[0]),
        pltpu.make_async_copy(
            direct_ref.at[pl.ds(own_rows, passed_rows), :], passed_hbm, left.at[1]
        ),
    ]
    for store in stores:
        store.start()
    gains_in.wait()
    gain_re = gains_ref[0]
    gain_im = gains_ref[1]
    parts = []
    for frame in range(frames_here + EARLY):
        direct = direct_ref[frame * inputs_here : (frame + 1) * inputs_here, :]
        direct_re = direct[:, :CH]
        direct_im = direct[:, CH:]
        parts.append(
            (
                gain_re * direct_re - gain_im * direct_im,
                gain_re * direct_im + gain_im * direct_re,
            )
        )
    slots = [
        [(part, frame) for frame in range(first, first + 8)]
        for first in range(0, frames_here, 8)
        for part in range(2)
    ]
    slots.append([(part, frames_here + frame) for part in range(2) for frame in range(EARLY)])
    per_far = CH // far
    for place, slot in enumerate(slots):
        columns = slice(place * LANES, (place + 1) * LANES)
        for half in range(CH // LANES):
            lanes = slice(half * LANES, (half + 1) * LANES)
            blocks = turn_granules([parts[frame][part][:, lanes] for part, frame in slot], per_far)
            for index in range(0, len(blocks), 2):
                row = place_in_column(half * len(blocks) + index, far) * inputs_here
                parcels_ref[row : row + 2 * inputs_here, columns] = jnp.concatenate(
                    blocks[index : index + 2], axis=0
                ).astype(jnp.bfloat16)
        lanes = pl.ds(place * LANES, LANES)
        stores.append(
            pltpu.make_async_copy(
                parcels_ref.at[:, lanes], parcels_hbm.at[:, lanes], left.at[len(stores)]
            )
        )
        stores[-1].start()
    for store in stores:
        store.wait()


def spectra_kernel(passed_ref, own_ref, gains_ref, spectra_ref, rows_ref):
    inputs_here = gains_ref.shape[1]
    frames_here = own_ref.shape[0] // inputs_here
    slabs = CH // LANES
    gain_re = gains_ref[0]
    gain_im = gains_ref[1]
    for frame in range(frames_here):
        block = slice(frame * inputs_here, (frame + 1) * inputs_here)
        direct = own_ref[block, :]
        if frame < TAPS - 1:
            direct = direct + passed_ref[block, :]
        direct_re = direct[:, :CH]
        direct_im = direct[:, CH:]
        rows = pl.ds(frame, inputs_here, stride=frames_here)
        real_part = gain_re * direct_re - gain_im * direct_im
        imag_part = gain_re * direct_im + gain_im * direct_re
        for slab in range(slabs):
            columns = slice(slab * LANES, (slab + 1) * LANES)
            rows_ref[slab, rows, :] = real_part[:, columns]
            rows_ref[slabs + slab, rows, :] = imag_part[:, columns]
    for part in range(2):
        for slab in range(slabs):
            columns = slice(slab * LANES, (slab + 1) * LANES)
            spectra_ref[part, :, columns] = rows_ref[part * slabs + slab].astype(jnp.bfloat16)


def channel_of(time):
    return time % 4


def place_in_plane(near, time, times):
    return (near + NEAR // 2) % NEAR * times + (time + times // 2) % times


def spread_kernel(mine_ref, parcels_ref, turned_ref):
    count, rows, width = parcels_ref.shape
    times = count // NEAR
    stride = mine_ref.shape[1] // rows
    for place in range(0, mine_ref.shape[1], LANES):
        values = mine_ref[:, place : place + LANES].astype(jnp.float32)
        turned_ref[place : place + LANES, :] = values.T
    for near in range(NEAR):
        for channel in range(stride // NEAR):
            start = near * (stride // NEAR) + channel
            values = turned_ref[pl.ds(start, rows, stride=stride), :].astype(jnp.bfloat16)
            for time in range(times):
                if channel_of(time) == channel:
                    parcels_ref[place_in_plane(near, time, times)] = values


def correlate_kernel(frames_all, inputs_here, place_ref, every_ref, packed_ref):
    count, lines, width = every_ref.shape
    blocks, rows, inputs_all = packed_ref.shape
    times = count // NEAR
    main = lines - 2 * EARLY
    carry = None
    lined = []
    for time in range(times):
        pieces = [every_ref[place_in_plane(near, time, times)] for near in range(NEAR)]
        wide = jnp.concatenate([piece.astype(jnp.float32) for piece in pieces], axis=1)
        tiles = [wide[start : start + 8] for start in range(0, lines, 8)]
        if carry is not None:
            early = lax.broadcasted_iota(jnp.int32, carry.shape, 0) < EARLY
            tiles[0] = tiles[0] + jnp.where(early, carry, 0.0)
            tiles[1] = tiles[1] + jnp.where(early, pltpu.roll(carry, 8 - EARLY, 0), 0.0)
        carry = tiles[-1]
        lined += tiles[:-1]
    far = width // inputs_here
    target = lax.broadcasted_iota(jnp.int32, (1, inputs_all), 1)
    near = target // inputs_here % NEAR
    listed = place_in_column(target // (inputs_here * NEAR), far)
    source = near * width + listed * inputs_here + target % inputs_here
    chosen = lax.broadcasted_iota(jnp.int32, (inputs_all, inputs_all), 0) == source
    ordered = jnp.dot(
        jnp.concatenate(lined, axis=0).astype(jnp.bfloat16),
        chosen.astype(jnp.float32).astype(jnp.bfloat16),
        preferred_element_type=jnp.float32,
    )
    right = ordered.astype(jnp.bfloat16)
    twisted = []
    for start in range(0, times * main, 16):
        twisted.append(ordered[start + 8 : start + 16])
        twisted.append(-ordered[start : start + 8])
    twisted = jnp.concatenate(twisted, axis=0).astype(jnp.bfloat16)
    held = blocks * rows
    first = place_ref[0] * held
    col_index = lax.broadcasted_iota(jnp.int32, (held, inputs_all), 1)
    row_index = lax.broadcasted_iota(jnp.int32, (held, inputs_all), 0) + first
    left = [jnp.where(first == 0, side[:, :held], side[:, held:]) for side in (right, twisted)]
    both = lax.dot_general(
        jnp.concatenate(left, axis=1),
        right,
        (((0,), (0,)), ((), ())),
        preferred_element_type=jnp.float32,
    )
    values = jnp.where(row_index <= col_index, both[:held], both[held:]) * (1.0 / frames_all)
    values = values.astype(jnp.bfloat16)
    for block in range(blocks):
        packed_ref[block] = values[block * rows : (block + 1) * rows]


def unpack_kernel(packed_ref, lines_hbm, lines_ref, left):
    channels, count, width = packed_ref.shape
    tiles = width // LANES
    stores = []
    for first in range(0, count, 16):
        start = first * tiles * channels
        for channel in range(channels):
            values = packed_ref[channel, first : first + 16, :].astype(jnp.float32)
            for tile in range(tiles):
                lines = pl.ds(start + tile * channels + channel, 16, stride=tiles * channels)
                lines_ref[lines, :] = values[:, tile * LANES : (tile + 1) * LANES]
        block = pl.ds(start, 16 * tiles * channels)
        stores.append(
            pltpu.make_async_copy(lines_ref.at[block, :], lines_hbm.at[block, :], left.at[len(stores)])
        )
        stores[-1].start()
    for store in stores:
        store.wait()


def body(samples, gains):
    inputs_here = samples.shape[0]
    frames_here = samples.shape[1] // NFFT
    times = lax.axis_size("tm")
    far = lax.axis_size("far")
    groups = far * NEAR
    per_group = CH // groups
    inputs_all = inputs_here * groups
    frames_all = frames_here * times
    block = inputs_here * frames_here

    window = filter_window()
    twiddle = jnp.asarray(build_table(window)[: NFFT // 2])
    window_taps = jnp.asarray(window.astype(np.float32).reshape(TAPS, NFFT))

    sent = frames_here + EARLY
    gains = gains.transpose(0, 2, 1)

    def own_part(*refs):
        own_part_kernel(far, *refs)

    own, passed, parcels = pl.pallas_call(
        own_part,
        out_shape=(
            jax.ShapeDtypeStruct((block, 2 * CH), jnp.float32),
            jax.ShapeDtypeStruct(((TAPS - 1) * inputs_here, 2 * CH), jnp.float32),
            jax.ShapeDtypeStruct((far * inputs_here, sent * 2 * CH // far), jnp.bfloat16),
        ),
        in_specs=[ANY] * 4,
        out_specs=(ANY, ANY, ANY),
        scratch_shapes=[
            pltpu.VMEM(samples.shape, jnp.bfloat16),
            pltpu.VMEM(window_taps.shape, jnp.float32),
            pltpu.VMEM(twiddle.shape, jnp.bfloat16),
            pltpu.VMEM(gains.shape, jnp.float32),
            pltpu.VMEM((sent * inputs_here, 2 * CH), jnp.float32),
            pltpu.VMEM((far * inputs_here, sent * 2 * CH // far), jnp.bfloat16),
            pltpu.SemaphoreType.DMA((3 + NFFT // (2 * STEP),)),
            pltpu.SemaphoreType.DMA((2 + sent // 4,)),
        ],
        compiler_params=pltpu.CompilerParams(vmem_limit_bytes=OWN_PART_VMEM),
        cost_estimate=pl.CostEstimate(
            flops=2 * sent * inputs_here * NFFT * 2 * CH,
            bytes_accessed=3 * 1024 * 1024,
            transcendentals=0,
        ),
        name="own_part",
    )(samples, window_taps, twiddle, gains)

    parcels = parcels.reshape(far, inputs_here, sent * 2 * CH // far)
    column = [sorted(range(far), key=lambda place: place_in_column(place, far))]
    mine = lax.all_to_all(parcels, "far", 0, 0, axis_index_groups=column)
    mine = mine.reshape(far * inputs_here, sent * 2 * CH // far)

    passed = lax.ppermute(passed, "tm", [(source, source + 1) for source in range(times - 1)])
    spectra = pl.pallas_call(
        spectra_kernel,
        out_shape=jax.ShapeDtypeStruct((2, block, CH), jnp.bfloat16),
        in_specs=[VMEM] * 3,
        out_specs=VMEM,
        scratch_shapes=[pltpu.VMEM((2 * CH // LANES, block, LANES), jnp.float32)],
        compiler_params=PARAMS,
        cost_estimate=pl.CostEstimate(
            flops=8 * block * 2 * CH, bytes_accessed=1024 * 1024, transcendentals=0
        ),
        name="spectra",
    )(passed, own, gains)
    mine, spectra = lax.optimization_barrier((mine, spectra))
    spectra = spectra.reshape(2, inputs_here, frames_here, CH).transpose(0, 3, 1, 2)

    lines = 2 * sent
    spread = pl.pallas_call(
        spread_kernel,
        out_shape=jax.ShapeDtypeStruct((NEAR * times, lines, far * inputs_here), jnp.bfloat16),
        in_specs=[VMEM],
        out_specs=VMEM,
        scratch_shapes=[pltpu.VMEM((sent * 2 * CH // far, far * inputs_here), jnp.float32)],
        compiler_params=PARAMS,
        name="spread",
    )(mine)
    place = lax.axis_index("tm").astype(jnp.int32)
    square = (place // 4)[None]
    spread, square = lax.optimization_barrier((spread, square))
    members = [(near, time) for near in range(NEAR) for time in range(times)]
    members.sort(key=lambda member: place_in_plane(*member, times))
    plane = [[near * times + time for near, time in members]]
    every = lax.all_to_all(spread, ("near", "tm"), 0, 0, axis_index_groups=plane)

    def correlate(*refs):
        correlate_kernel(frames_all, inputs_here, *refs)

    rows = inputs_all // times
    packed = pl.pallas_call(
        correlate,
        out_shape=jax.ShapeDtypeStruct((per_group, rows, inputs_all), jnp.bfloat16),
        in_specs=[SMEM, VMEM],
        out_specs=VMEM,
        compiler_params=PARAMS,
        name="correlate",
    )(square, every)
    squares = [[0, 1, 2, 3], [4, 5, 6, 7]]
    packed = lax.all_to_all(packed, "tm", 0, 0, axis_index_groups=squares)
    tiles = inputs_all // LANES
    visibilities = pl.pallas_call(
        unpack_kernel,
        out_shape=jax.ShapeDtypeStruct((rows * tiles * per_group, LANES), jnp.float32),
        in_specs=[VMEM],
        out_specs=ANY,
        scratch_shapes=[
            pltpu.VMEM((rows * tiles * per_group, LANES), jnp.float32),
            pltpu.SemaphoreType.DMA((rows // 16,)),
        ],
        compiler_params=PARAMS,
        name="unpack",
    )(packed)
    visibilities = visibilities.reshape(rows, tiles, per_group, LANES).transpose(0, 2, 1, 3)
    visibilities = visibilities.reshape(rows, per_group, inputs_all)
    return (spectra, visibilities)


def solution(mesh):
    groups, times = mesh.devices.shape
    split = Mesh(mesh.devices.reshape(groups // NEAR, NEAR, times), ("far", "near", "tm"))
    inputs = ("far", "near")
    return jax.shard_map(
        body,
        mesh=split,
        in_specs=(P(inputs, "tm"), P(None, None, inputs)),
        out_specs=(P(None, None, inputs, "tm"), P("tm", inputs, None)),
        check_vma=False,
    )
```

profile of v0, /device:TPU:6, one launch (start us, length us, event | category | flops | bytes accessed | tf_op | source)
XLA Modules:
  0.0 54.3 jit_solution(18317083508229320424)
XLA Ops:
  0.6 2.9 %own_part.1 = (f32[128,512]{1,0:T(8,128)}, f32[24,512]{1,0:T(8,128)}, bf16[128,640]{1,0:T(8,128)(2,1)}) custom-call(bf16[8,32768]{1,0:T(8,128)(2,1)} %refs_0_.1, f32[4,2048]{1,0:T(4,128)} %constant.25.clone.refs_1_, bf16[1024,512]{1,0:T(8,128)(2,1)} %constant.24.clone.refs_2_, f32[2,8,256]{2,1,0:T(8,128)} %bitcast.13), custom_call_target="tpu_custom_call" | custom-call | flops 335544320 | bytes 3145728 | tf_op jit(solution)/shard_map/own_part/pallas_call | solution.py:337
  3.5 0.0 copy-start
  3.5 0.0 copy-start.2
  3.5 17.2 %all-to-all-start = ((bf16[16,8,640]{2,1,0:T(8,128)(2,1)}), bf16[16,8,640]{2,1,0:T(8,128)(2,1)S(1)}, u32[]{:S(2)}, u32[]{:S(2)}) async-start(bf16[16,8,640]{2,1,0:T(8,128)(2,1)} %bitcast.16), calls=%async_computation | async-start | bytes 327680 | tf_op jit(solution)/shard_map/all_to_all | solution.py:367
  20.7 0.0 copy-done.2
  20.7 3.5 %collective-permute-start = (f32[24,512]{1,0:T(8,128)S(1)}, f32[24,512]{1,0:T(8,128)S(1)}, u32[]{:S(2)}, u32[]{:S(2)}) collective-permute-start(f32[24,512]{1,0:T(8,128)S(1)} %copy-done.2), channel_id=1, source_target_pairs={{0,1},{1,2},{2,3},{3,4},{4,5},{5,6},{6,7},{8,9},{9,10},{10,11},{11... | collective-permute-start | bytes 147464 | tf_op jit(solution)/shard_map/ppermute | solution.py:370
  24.2 0.0 copy-start.1
  24.2 3.4 %collective-permute-done.passed_ref = f32[24,512]{1,0:T(8,128)S(1)} collective-permute-done((f32[24,512]{1,0:T(8,128)S(1)}, f32[24,512]{1,0:T(8,128)S(1)}, u32[]{:S(2)}, u32[]{:S(2)}) %collective-permute-start) | collective-permute-done | bytes 49184 | tf_op jit(solution)/shard_map/ppermute | solution.py:370
  27.6 0.0 copy-done
  27.6 0.0 copy-done.1
  27.6 0.8 %spectra.1 = bf16[2,128,256]{2,1,0:T(8,128)(2,1)} custom-call(f32[24,512]{1,0:T(8,128)S(1)} %collective-permute-done.passed_ref, f32[128,512]{1,0:T(8,128)S(1)} %copy-done, f32[2,8,256]{2,1,0:T(8,128)S(1)} %bitcast.14), custom_call_target="tpu_custom_call" | custom-call | flops 524288 | bytes 1048576 | tf_op jit(solution)/shard_map/spectra/pallas_call | solution.py:371
  28.4 1.9 %all-to-all-done = bf16[16,8,640]{2,1,0:T(8,128)(2,1)S(1)} async-done(((bf16[16,8,640]{2,1,0:T(8,128)(2,1)}), bf16[16,8,640]{2,1,0:T(8,128)(2,1)S(1)}, u32[]{:S(2)}, u32[]{:S(2)}) %all-to-all-start) | async-done | bytes 163872 | tf_op jit(solution)/shard_map/all_to_all | solution.py:367
  30.3 0.2 spread.1
  30.5 13.6 %all_to_all.15.refs_1_ = bf16[32,40,128]{2,1,0:T(8,128)(2,1)S(1)} all-to-all(bf16[32,40,128]{2,1,0:T(8,128)(2,1)S(1)} %spread.1), channel_id=1, replica_groups={{20,21,22,23,16,17,18,19,28,29,30,31,24,25,26,27,4,5,6,7,0,1,2,3,12,13,..., dimensions={0} | all-to-all | bytes 655360 | tf_op jit(solution)/shard_map/all_to_all | solution.py:402
  44.1 0.6 %correlate.1 = bf16[4,64,512]{2,1,0:T(8,128)(2,1)S(1)} custom-call(s32[1]{0:T(128)} %bitcast.5.refs_0_, bf16[32,40,128]{2,1,0:T(8,128)(2,1)S(1)} %all_to_all.15.refs_1_), custom_call_target="tpu_custom_call" | custom-call | tf_op jit(solution)/shard_map/correlate/pallas_call | solution.py:408
  44.7 8.7 %all_to_all.16.packed_ref = bf16[4,64,512]{2,1,0:T(8,128)(2,1)S(1)} all-to-all(bf16[4,64,512]{2,1,0:T(8,128)(2,1)S(1)} %correlate.1), channel_id=1, replica_groups={{0,1,2,3},{4,5,6,7},{8,9,10,11},{12,13,14,15},{16,17,18,19},{20,21,22,2..., dimensions={0} | all-to-all | bytes 524288 | tf_op jit(solution)/shard_map/all_to_all | solution.py:417
  53.4 0.9 %unpack.1 = f32[1024,128]{1,0:T(8,128)} custom-call(bf16[4,64,512]{2,1,0:T(8,128)(2,1)S(1)} %all_to_all.16.packed_ref), custom_call_target="tpu_custom_call" | custom-call | tf_op jit(solution)/shard_map/unpack/pallas_call | solution.py:419
Async XLA Ops:
  3.5 24.1 %copy-start = (f32[128,512]{1,0:T(8,128)S(1)}, f32[128,512]{1,0:T(8,128)}, u32[]{:S(2)}) copy-start(f32[128,512]{1,0:T(8,128)} %get-tuple-element.11.own_ref) | copy-start | bytes 786436
  3.5 17.2 %copy-start.2 = (f32[24,512]{1,0:T(8,128)S(1)}, f32[24,512]{1,0:T(8,128)}, u32[]{:S(2)}) copy-start(f32[24,512]{1,0:T(8,128)} %get-tuple-element.10) | copy-start | bytes 147460
  3.5 26.8 %all-to-all-start = ((bf16[16,8,640]{2,1,0:T(8,128)(2,1)}), bf16[16,8,640]{2,1,0:T(8,128)(2,1)S(1)}, u32[]{:S(2)}, u32[]{:S(2)}) async-start(bf16[16,8,640]{2,1,0:T(8,128)(2,1)} %bitcast.16), calls=%async_computation | async-start | bytes 327680 | tf_op jit(solution)/shard_map/all_to_all | solution.py:367
  20.7 6.9 %collective-permute-start = (f32[24,512]{1,0:T(8,128)S(1)}, f32[24,512]{1,0:T(8,128)S(1)}, u32[]{:S(2)}, u32[]{:S(2)}) collective-permute-start(f32[24,512]{1,0:T(8,128)S(1)} %copy-done.2), channel_id=1, source_target_pairs={{0,1},{1,2},{2,3},{3,4},{4,5},{5,6},{6,7},{8,9},{9,10},{10,11},{11... | collective-permute-start | bytes 147464 | tf_op jit(solution)/shard_map/ppermute | solution.py:370
  24.2 3.4 %copy-start.1 = (f32[2,256,8]{1,2,0:T(8,128)S(1)}, f32[2,256,8]{1,2,0:T(8,128)}, u32[]{:S(2)}) copy-start(f32[2,256,8]{1,2,0:T(8,128)} %param.5) | copy-start | bytes 49156
where the time goes:
time: 54.9 us; the launch traced here: 54.3 us
  blocking collectives  22.3 us (41%)
  starting transfers between devices  20.7 us (38%)
  Pallas kernels  5.36 us (10%)
  waiting for transfers between devices  5.24 us (10%)
  between operations  0.71 us (1%)
    all_to_all x1, starting transfers between devices, body(): mine = lax.all_to_all(parcels, 'far', 0, 0, axis_index_groups=column)  17.2 us
    all_to_all x1, blocking collectives, body(): lax.all_to_all(spread, ('near', 'tm'), 0, 0, axis_index_groups=plane)  13.6 us
    all_to_all x1, blocking collectives, body(): packed = lax.all_to_all(packed, 'tm', 0, 0, axis_index_groups=squares)  8.71 us
    ppermute x1, starting transfers between devices, body(): lax.ppermute(passed, 'tm', [(source, source + 1) for source in range(time...  3.49 us
    ppermute x1, waiting for transfers between devices, body(): lax.ppermute(passed, 'tm', [(source, source + 1) for source in range(time...  3.36 us
    pallas_call x1, Pallas kernels, body(): pl.pallas_call(own_part, out_shape=(jax.ShapeDtypeStruct((block, 2 * CH),...  2.86 us
    all_to_all x1, waiting for transfers between devices, body(): mine = lax.all_to_all(parcels, 'far', 0, 0, axis_index_groups=column)  1.88 us
  transfers between devices with their start and end apart: 2, of which 2 were waited for; matrix products, arithmetic and copies ran while one was open for 0% of the time, Pallas kernels for 1%

commit v1 on v0

--- a/solution.py
+++ b/solution.py
@@ -83,7 +83,7 @@
 
 
 def place_in_column(place, far):
-    return (place + far * 3 // 8) % far
+    return (far * 5 // 8 + far - place) % far
 
 
 def own_part_kernel(
@@ -173,14 +173,16 @@
     per_far = CH // far
     for place, slot in enumerate(slots):
         columns = slice(place * LANES, (place + 1) * LANES)
+        blocks = []
         for half in range(CH // LANES):
             lanes = slice(half * LANES, (half + 1) * LANES)
-            blocks = turn_granules([parts[frame][part][:, lanes] for part, frame in slot], per_far)
-            for index in range(0, len(blocks), 2):
-                row = place_in_column(half * len(blocks) + index, far) * inputs_here
-                parcels_ref[row : row + 2 * inputs_here, columns] = jnp.concatenate(
-                    blocks[index : index + 2], axis=0
-                ).astype(jnp.bfloat16)
+            blocks += turn_granules([parts[frame][part][:, lanes] for part, frame in slot], per_far)
+        listed = sorted(range(far), key=lambda target: place_in_column(target, far))
+        for index in range(0, far, 2):
+            rows = slice(index * inputs_here, (index + 2) * inputs_here)
+            parcels_ref[rows, columns] = jnp.concatenate(
+                [blocks[target] for target in listed[index : index + 2]], axis=0
+            ).astype(jnp.bfloat16)
         lanes = pl.ds(place * LANES, LANES)
         stores.append(
             pltpu.make_async_copy(

time: 54.9 us -> 55 us (level)
  no operation moved by 1% of the time
where the time goes in v1:
time: 55 us; the launch traced here: 54.4 us
  blocking collectives  22.3 us (41%)
  starting transfers between devices  20.7 us (38%)
  waiting for transfers between devices  5.39 us (10%)
  Pallas kernels  5.36 us (10%)
  between operations  0.71 us (1%)
    all_to_all x1, starting transfers between devices, body(): mine = lax.all_to_all(parcels, 'far', 0, 0, axis_index_groups=column)  17.2 us
    all_to_all x1, blocking collectives, body(): lax.all_to_all(spread, ('near', 'tm'), 0, 0, axis_index_groups=plane)  13.6 us
    all_to_all x1, blocking collectives, body(): packed = lax.all_to_all(packed, 'tm', 0, 0, axis_index_groups=squares)  8.71 us
    ppermute x1, starting transfers between devices, body(): lax.ppermute(passed, 'tm', [(source, source + 1) for source in range(time...  3.49 us
    ppermute x1, waiting for transfers between devices, body(): lax.ppermute(passed, 'tm', [(source, source + 1) for source in range(time...  3.36 us
    pallas_call x1, Pallas kernels, body(): pl.pallas_call(own_part, out_shape=(jax.ShapeDtypeStruct((block, 2 * CH),...  2.86 us
    all_to_all x1, waiting for transfers between devices, body(): mine = lax.all_to_all(parcels, 'far', 0, 0, axis_index_groups=column)  2.02 us
  transfers between devices with their start and end apart: 2, of which 2 were waited for; matrix products, arithmetic and copies ran while one was open for 0% of the time, Pallas kernels for 1%

profile of v1, /device:TPU:6, one launch (start us, length us, event | category | flops | bytes accessed | tf_op | source)
XLA Modules:
  0.0 54.4 jit_solution(738705110735540393)
XLA Ops:
  0.6 2.9 %own_part.1 = (f32[128,512]{1,0:T(8,128)}, f32[24,512]{1,0:T(8,128)}, bf16[128,640]{1,0:T(8,128)(2,1)}) custom-call(bf16[8,32768]{1,0:T(8,128)(2,1)} %refs_0_.1, f32[4,2048]{1,0:T(4,128)} %constant.25.clone.refs_1_, bf16[1024,512]{1,0:T(8,128)(2,1)} %constant.24.clone.refs_2_, f32[2,8,256]{2,1,0:T(8,128)} %bitcast.13), custom_call_target="tpu_custom_call" | custom-call | flops 335544320 | bytes 3145728 | tf_op jit(solution)/shard_map/own_part/pallas_call | solution.py:339
  3.5 0.0 copy-start
  3.5 0.0 copy-start.2
  3.5 17.2 %all-to-all-start = ((bf16[16,8,640]{2,1,0:T(8,128)(2,1)}), bf16[16,8,640]{2,1,0:T(8,128)(2,1)S(1)}, u32[]{:S(2)}, u32[]{:S(2)}) async-start(bf16[16,8,640]{2,1,0:T(8,128)(2,1)} %bitcast.16), calls=%async_computation | async-start | bytes 327680 | tf_op jit(solution)/shard_map/all_to_all | solution.py:369
  20.7 0.0 copy-done.2
  20.7 3.5 %collective-permute-start = (f32[24,512]{1,0:T(8,128)S(1)}, f32[24,512]{1,0:T(8,128)S(1)}, u32[]{:S(2)}, u32[]{:S(2)}) collective-permute-start(f32[24,512]{1,0:T(8,128)S(1)} %copy-done.2), channel_id=1, source_target_pairs={{0,1},{1,2},{2,3},{3,4},{4,5},{5,6},{6,7},{8,9},{9,10},{10,11},{11... | collective-permute-start | bytes 147464 | tf_op jit(solution)/shard_map/ppermute | solution.py:372
  24.2 0.0 copy-start.1
  24.2 3.4 %collective-permute-done.passed_ref = f32[24,512]{1,0:T(8,128)S(1)} collective-permute-done((f32[24,512]{1,0:T(8,128)S(1)}, f32[24,512]{1,0:T(8,128)S(1)}, u32[]{:S(2)}, u32[]{:S(2)}) %collective-permute-start) | collective-permute-done | bytes 49184 | tf_op jit(solution)/shard_map/ppermute | solution.py:372
  27.6 0.0 copy-done
  27.6 0.0 copy-done.1
  27.6 0.8 %spectra.1 = bf16[2,128,256]{2,1,0:T(8,128)(2,1)} custom-call(f32[24,512]{1,0:T(8,128)S(1)} %collective-permute-done.passed_ref, f32[128,512]{1,0:T(8,128)S(1)} %copy-done, f32[2,8,256]{2,1,0:T(8,128)S(1)} %bitcast.14), custom_call_target="tpu_custom_call" | custom-call | flops 524288 | bytes 1048576 | tf_op jit(solution)/shard_map/spectra/pallas_call | solution.py:373
  28.4 2.0 %all-to-all-done = bf16[16,8,640]{2,1,0:T(8,128)(2,1)S(1)} async-done(((bf16[16,8,640]{2,1,0:T(8,128)(2,1)}), bf16[16,8,640]{2,1,0:T(8,128)(2,1)S(1)}, u32[]{:S(2)}, u32[]{:S(2)}) %all-to-all-start) | async-done | bytes 163872 | tf_op jit(solution)/shard_map/all_to_all | solution.py:369
  30.4 0.2 spread.1
  30.6 13.6 %all_to_all.15.refs_1_ = bf16[32,40,128]{2,1,0:T(8,128)(2,1)S(1)} all-to-all(bf16[32,40,128]{2,1,0:T(8,128)(2,1)S(1)} %spread.1), channel_id=1, replica_groups={{20,21,22,23,16,17,18,19,28,29,30,31,24,25,26,27,4,5,6,7,0,1,2,3,12,13,..., dimensions={0} | all-to-all | bytes 655360 | tf_op jit(solution)/shard_map/all_to_all | solution.py:404
  44.2 0.6 %correlate.1 = bf16[4,64,512]{2,1,0:T(8,128)(2,1)S(1)} custom-call(s32[1]{0:T(128)} %bitcast.5.refs_0_, bf16[32,40,128]{2,1,0:T(8,128)(2,1)S(1)} %all_to_all.15.refs_1_), custom_call_target="tpu_custom_call" | custom-call | tf_op jit(solution)/shard_map/correlate/pallas_call | solution.py:410
  44.8 8.7 %all_to_all.16.packed_ref = bf16[4,64,512]{2,1,0:T(8,128)(2,1)S(1)} all-to-all(bf16[4,64,512]{2,1,0:T(8,128)(2,1)S(1)} %correlate.1), channel_id=1, replica_groups={{0,1,2,3},{4,5,6,7},{8,9,10,11},{12,13,14,15},{16,17,18,19},{20,21,22,2..., dimensions={0} | all-to-all | bytes 524288 | tf_op jit(solution)/shard_map/all_to_all | solution.py:419
  53.6 0.9 %unpack.1 = f32[1024,128]{1,0:T(8,128)} custom-call(bf16[4,64,512]{2,1,0:T(8,128)(2,1)S(1)} %all_to_all.16.packed_ref), custom_call_target="tpu_custom_call" | custom-call | tf_op jit(solution)/shard_map/unpack/pallas_call | solution.py:421
Async XLA Ops:
  3.5 24.1 %copy-start = (f32[128,512]{1,0:T(8,128)S(1)}, f32[128,512]{1,0:T(8,128)}, u32[]{:S(2)}) copy-start(f32[128,512]{1,0:T(8,128)} %get-tuple-element.11.own_ref) | copy-start | bytes 786436
  3.5 17.2 %copy-start.2 = (f32[24,512]{1,0:T(8,128)S(1)}, f32[24,512]{1,0:T(8,128)}, u32[]{:S(2)}) copy-start(f32[24,512]{1,0:T(8,128)} %get-tuple-element.10) | copy-start | bytes 147460
  3.5 26.9 %all-to-all-start = ((bf16[16,8,640]{2,1,0:T(8,128)(2,1)}), bf16[16,8,640]{2,1,0:T(8,128)(2,1)S(1)}, u32[]{:S(2)}, u32[]{:S(2)}) async-start(bf16[16,8,640]{2,1,0:T(8,128)(2,1)} %bitcast.16), calls=%async_computation | async-start | bytes 327680 | tf_op jit(solution)/shard_map/all_to_all | solution.py:369
  20.7 6.9 %collective-permute-start = (f32[24,512]{1,0:T(8,128)S(1)}, f32[24,512]{1,0:T(8,128)S(1)}, u32[]{:S(2)}, u32[]{:S(2)}) collective-permute-start(f32[24,512]{1,0:T(8,128)S(1)} %copy-done.2), channel_id=1, source_target_pairs={{0,1},{1,2},{2,3},{3,4},{4,5},{5,6},{6,7},{8,9},{9,10},{10,11},{11... | collective-permute-start | bytes 147464 | tf_op jit(solution)/shard_map/ppermute | solution.py:372
  24.2 3.4 %copy-start.1 = (f32[2,256,8]{1,2,0:T(8,128)S(1)}, f32[2,256,8]{1,2,0:T(8,128)}, u32[]{:S(2)}) copy-start(f32[2,256,8]{1,2,0:T(8,128)} %param.5) | copy-start | bytes 49156

commit v2 on v1

--- a/solution.py
+++ b/solution.py
@@ -217,7 +217,8 @@
     for part in range(2):
         for slab in range(slabs):
             columns = slice(slab * LANES, (slab + 1) * LANES)
-            spectra_ref[part, :, columns] = rows_ref[part * slabs + slab].astype(jnp.bfloat16)
+            values = rows_ref[part * slabs + slab, : own_ref.shape[0], :]
+            spectra_ref[part, :, columns] = values.astype(jnp.bfloat16)
 
 
 def channel_of(time):
@@ -225,7 +226,9 @@
 
 
 def place_in_plane(near, time, times):
-    return (near + NEAR // 2) % NEAR * times + (time + times // 2) % times
+    count = NEAR * times
+    middle = NEAR // 2 * times + times // 2
+    return 3 * (near * times + time + count - middle) % count
 
 
 def spread_kernel(mine_ref, parcels_ref, turned_ref):
@@ -375,7 +378,7 @@
         out_shape=jax.ShapeDtypeStruct((2, block, CH), jnp.bfloat16),
         in_specs=[VMEM] * 3,
         out_specs=VMEM,
-        scratch_shapes=[pltpu.VMEM((2 * CH // LANES, block, LANES), jnp.float32)],
+        scratch_shapes=[pltpu.VMEM((2 * CH // LANES, block + frames_here, LANES), jnp.float32)],
         compiler_params=PARAMS,
         cost_estimate=pl.CostEstimate(
             flops=8 * block * 2 * CH, bytes_accessed=1024 * 1024, transcendentals=0
@@ -391,7 +394,7 @@
         out_shape=jax.ShapeDtypeStruct((NEAR * times, lines, far * inputs_here), jnp.bfloat16),
         in_specs=[VMEM],
         out_specs=VMEM,
-        scratch_shapes=[pltpu.VMEM((sent * 2 * CH // far, far * inputs_here), jnp.float32)],
+        scratch_shapes=[pltpu.VMEM(((sent + 1) * 2 * CH // far, far * inputs_here), jnp.float32)],
         compiler_params=PARAMS,
         name="spread",
     )(mine)
@@ -424,7 +427,7 @@
         in_specs=[VMEM],
         out_specs=ANY,
         scratch_shapes=[
-            pltpu.VMEM((rows * tiles * per_group, LANES), jnp.float32),
+            pltpu.VMEM(((rows + 1) * tiles * per_group, LANES), jnp.float32),
             pltpu.SemaphoreType.DMA((rows // 16,)),
         ],
         compiler_params=PARAMS,

time: 55 us -> 54.8 us (level)
  no operation moved by 1% of the time
where the time goes in v2:
time: 54.8 us; the launch traced here: 54.2 us
  blocking collectives  22.1 us (40%)
  starting transfers between devices  20.7 us (38%)
  waiting for transfers between devices  5.39 us (10%)
  Pallas kernels  5.36 us (10%)
  between operations  0.71 us (1%)
    all_to_all x1, starting transfers between devices, body(): mine = lax.all_to_all(parcels, 'far', 0, 0, axis_index_groups=column)  17.2 us
    all_to_all x1, blocking collectives, body(): lax.all_to_all(spread, ('near', 'tm'), 0, 0, axis_index_groups=plane)  13.2 us
    all_to_all x1, blocking collectives, body(): packed = lax.all_to_all(packed, 'tm', 0, 0, axis_index_groups=squares)  8.92 us
    ppermute x1, starting transfers between devices, body(): lax.ppermute(passed, 'tm', [(source, source + 1) for source in range(time...  3.49 us
    ppermute x1, waiting for transfers between devices, body(): lax.ppermute(passed, 'tm', [(source, source + 1) for source in range(time...  3.36 us
    pallas_call x1, Pallas kernels, body(): pl.pallas_call(own_part, out_shape=(jax.ShapeDtypeStruct((block, 2 * CH),...  2.86 us
    all_to_all x1, waiting for transfers between devices, body(): mine = lax.all_to_all(parcels, 'far', 0, 0, axis_index_groups=column)  2.02 us
  transfers between devices with their start and end apart: 2, of which 2 were waited for; matrix products, arithmetic and copies ran while one was open for 0% of the time, Pallas kernels for 1%

profile of v2, /device:TPU:6, one launch (start us, length us, event | category | flops | bytes accessed | tf_op | source)
XLA Modules:
  0.0 54.2 jit_solution(11927970962722129767)
XLA Ops:
  0.6 2.9 %own_part.1 = (f32[128,512]{1,0:T(8,128)}, f32[24,512]{1,0:T(8,128)}, bf16[128,640]{1,0:T(8,128)(2,1)}) custom-call(bf16[8,32768]{1,0:T(8,128)(2,1)} %refs_0_.1, f32[4,2048]{1,0:T(4,128)} %constant.25.clone.refs_1_, bf16[1024,512]{1,0:T(8,128)(2,1)} %constant.24.clone.refs_2_, f32[2,8,256]{2,1,0:T(8,128)} %bitcast.13), custom_call_target="tpu_custom_call" | custom-call | flops 335544320 | bytes 3145728 | tf_op jit(solution)/shard_map/own_part/pallas_call | solution.py:342
  3.5 0.0 copy-start
  3.5 0.0 copy-start.2
  3.5 17.2 %all-to-all-start = ((bf16[16,8,640]{2,1,0:T(8,128)(2,1)}), bf16[16,8,640]{2,1,0:T(8,128)(2,1)S(1)}, u32[]{:S(2)}, u32[]{:S(2)}) async-start(bf16[16,8,640]{2,1,0:T(8,128)(2,1)} %bitcast.16), calls=%async_computation | async-start | bytes 327680 | tf_op jit(solution)/shard_map/all_to_all | solution.py:372
  20.7 0.0 copy-done.2
  20.7 3.5 %collective-permute-start = (f32[24,512]{1,0:T(8,128)S(1)}, f32[24,512]{1,0:T(8,128)S(1)}, u32[]{:S(2)}, u32[]{:S(2)}) collective-permute-start(f32[24,512]{1,0:T(8,128)S(1)} %copy-done.2), channel_id=1, source_target_pairs={{0,1},{1,2},{2,3},{3,4},{4,5},{5,6},{6,7},{8,9},{9,10},{10,11},{11... | collective-permute-start | bytes 147464 | tf_op jit(solution)/shard_map/ppermute | solution.py:375
  24.2 0.0 copy-start.1
  24.2 3.4 %collective-permute-done.passed_ref = f32[24,512]{1,0:T(8,128)S(1)} collective-permute-done((f32[24,512]{1,0:T(8,128)S(1)}, f32[24,512]{1,0:T(8,128)S(1)}, u32[]{:S(2)}, u32[]{:S(2)}) %collective-permute-start) | collective-permute-done | bytes 49184 | tf_op jit(solution)/shard_map/ppermute | solution.py:375
  27.6 0.0 copy-done
  27.6 0.0 copy-done.1
  27.6 0.8 %spectra.1 = bf16[2,128,256]{2,1,0:T(8,128)(2,1)} custom-call(f32[24,512]{1,0:T(8,128)S(1)} %collective-permute-done.passed_ref, f32[128,512]{1,0:T(8,128)S(1)} %copy-done, f32[2,8,256]{2,1,0:T(8,128)S(1)} %bitcast.14), custom_call_target="tpu_custom_call" | custom-call | flops 524288 | bytes 1048576 | tf_op jit(solution)/shard_map/spectra/pallas_call | solution.py:376
  28.4 2.0 %all-to-all-done = bf16[16,8,640]{2,1,0:T(8,128)(2,1)S(1)} async-done(((bf16[16,8,640]{2,1,0:T(8,128)(2,1)}), bf16[16,8,640]{2,1,0:T(8,128)(2,1)S(1)}, u32[]{:S(2)}, u32[]{:S(2)}) %all-to-all-start) | async-done | bytes 163872 | tf_op jit(solution)/shard_map/all_to_all | solution.py:372
  30.4 0.2 spread.1
  30.6 13.2 %all_to_all.15.refs_1_ = bf16[32,40,128]{2,1,0:T(8,128)(2,1)S(1)} all-to-all(bf16[32,40,128]{2,1,0:T(8,128)(2,1)S(1)} %spread.1), channel_id=1, replica_groups={{20,31,10,21,0,11,22,1,12,23,2,13,24,3,14,25,4,15,26,5,16,27,6,17,28,7,..., dimensions={0} | all-to-all | bytes 655360 | tf_op jit(solution)/shard_map/all_to_all | solution.py:407
  43.8 0.6 %correlate.1 = bf16[4,64,512]{2,1,0:T(8,128)(2,1)S(1)} custom-call(s32[1]{0:T(128)} %bitcast.5.refs_0_, bf16[32,40,128]{2,1,0:T(8,128)(2,1)S(1)} %all_to_all.15.refs_1_), custom_call_target="tpu_custom_call" | custom-call | tf_op jit(solution)/shard_map/correlate/pallas_call | solution.py:413
  44.5 8.9 %all_to_all.16.packed_ref = bf16[4,64,512]{2,1,0:T(8,128)(2,1)S(1)} all-to-all(bf16[4,64,512]{2,1,0:T(8,128)(2,1)S(1)} %correlate.1), channel_id=1, replica_groups={{0,1,2,3},{4,5,6,7},{8,9,10,11},{12,13,14,15},{16,17,18,19},{20,21,22,2..., dimensions={0} | all-to-all | bytes 524288 | tf_op jit(solution)/shard_map/all_to_all | solution.py:422
  53.4 0.9 %unpack.1 = f32[1024,128]{1,0:T(8,128)} custom-call(bf16[4,64,512]{2,1,0:T(8,128)(2,1)S(1)} %all_to_all.16.packed_ref), custom_call_target="tpu_custom_call" | custom-call | tf_op jit(solution)/shard_map/unpack/pallas_call | solution.py:424
Async XLA Ops:
  3.5 24.1 %copy-start = (f32[128,512]{1,0:T(8,128)S(1)}, f32[128,512]{1,0:T(8,128)}, u32[]{:S(2)}) copy-start(f32[128,512]{1,0:T(8,128)} %get-tuple-element.11.own_ref) | copy-start | bytes 786436
  3.5 17.2 %copy-start.2 = (f32[24,512]{1,0:T(8,128)S(1)}, f32[24,512]{1,0:T(8,128)}, u32[]{:S(2)}) copy-start(f32[24,512]{1,0:T(8,128)} %get-tuple-element.10) | copy-start | bytes 147460
  3.5 26.9 %all-to-all-start = ((bf16[16,8,640]{2,1,0:T(8,128)(2,1)}), bf16[16,8,640]{2,1,0:T(8,128)(2,1)S(1)}, u32[]{:S(2)}, u32[]{:S(2)}) async-start(bf16[16,8,640]{2,1,0:T(8,128)(2,1)} %bitcast.16), calls=%async_computation | async-start | bytes 327680 | tf_op jit(solution)/shard_map/all_to_all | solution.py:372
  20.7 6.9 %collective-permute-start = (f32[24,512]{1,0:T(8,128)S(1)}, f32[24,512]{1,0:T(8,128)S(1)}, u32[]{:S(2)}, u32[]{:S(2)}) collective-permute-start(f32[24,512]{1,0:T(8,128)S(1)} %copy-done.2), channel_id=1, source_target_pairs={{0,1},{1,2},{2,3},{3,4},{4,5},{5,6},{6,7},{8,9},{9,10},{10,11},{11... | collective-permute-start | bytes 147464 | tf_op jit(solution)/shard_map/ppermute | solution.py:375
  24.2 3.4 %copy-start.1 = (f32[2,256,8]{1,2,0:T(8,128)S(1)}, f32[2,256,8]{1,2,0:T(8,128)}, u32[]{:S(2)}) copy-start(f32[2,256,8]{1,2,0:T(8,128)} %param.5) | copy-start | bytes 49156

commit v3 on v2

--- a/solution.py
+++ b/solution.py
@@ -83,7 +83,7 @@
 
 
 def place_in_column(place, far):
-    return (far * 5 // 8 + far - place) % far
+    return (place + far * 3 // 8) % far
 
 
 def own_part_kernel(

time: 54.8 us -> 54.7 us (level)
  no operation moved by 1% of the time
where the time goes in v3:
time: 54.7 us; the launch traced here: 54.1 us
  blocking collectives  22.1 us (40%)
  starting transfers between devices  20.7 us (38%)
  Pallas kernels  5.36 us (10%)
  waiting for transfers between devices  5.24 us (10%)
  between operations  0.71 us (1%)
    all_to_all x1, starting transfers between devices, body(): mine = lax.all_to_all(parcels, 'far', 0, 0, axis_index_groups=column)  17.2 us
    all_to_all x1, blocking collectives, body(): lax.all_to_all(spread, ('near', 'tm'), 0, 0, axis_index_groups=plane)  13.2 us
    all_to_all x1, blocking collectives, body(): packed = lax.all_to_all(packed, 'tm', 0, 0, axis_index_groups=squares)  8.93 us
    ppermute x1, starting transfers between devices, body(): lax.ppermute(passed, 'tm', [(source, source + 1) for source in range(time...  3.49 us
    ppermute x1, waiting for transfers between devices, body(): lax.ppermute(passed, 'tm', [(source, source + 1) for source in range(time...  3.36 us
    pallas_call x1, Pallas kernels, body(): pl.pallas_call(own_part, out_shape=(jax.ShapeDtypeStruct((block, 2 * CH),...  2.86 us
    all_to_all x1, waiting for transfers between devices, body(): mine = lax.all_to_all(parcels, 'far', 0, 0, axis_index_groups=column)  1.87 us
  transfers between devices with their start and end apart: 2, of which 2 were waited for; matrix products, arithmetic and copies ran while one was open for 0% of the time, Pallas kernels for 1%

profile of v3, /device:TPU:6, one launch (start us, length us, event | category | flops | bytes accessed | tf_op | source)
XLA Modules:
  0.0 54.1 jit_solution(10635325423008516651)
XLA Ops:
  0.6 2.9 %own_part.1 = (f32[128,512]{1,0:T(8,128)}, f32[24,512]{1,0:T(8,128)}, bf16[128,640]{1,0:T(8,128)(2,1)}) custom-call(bf16[8,32768]{1,0:T(8,128)(2,1)} %refs_0_.1, f32[4,2048]{1,0:T(4,128)} %constant.25.clone.refs_1_, bf16[1024,512]{1,0:T(8,128)(2,1)} %constant.24.clone.refs_2_, f32[2,8,256]{2,1,0:T(8,128)} %bitcast.13), custom_call_target="tpu_custom_call" | custom-call | flops 335544320 | bytes 3145728 | tf_op jit(solution)/shard_map/own_part/pallas_call | solution.py:342
  3.5 0.0 copy-start
  3.5 0.0 copy-start.2
  3.5 17.2 %all-to-all-start = ((bf16[16,8,640]{2,1,0:T(8,128)(2,1)}), bf16[16,8,640]{2,1,0:T(8,128)(2,1)S(1)}, u32[]{:S(2)}, u32[]{:S(2)}) async-start(bf16[16,8,640]{2,1,0:T(8,128)(2,1)} %bitcast.16), calls=%async_computation | async-start | bytes 327680 | tf_op jit(solution)/shard_map/all_to_all | solution.py:372
  20.7 0.0 copy-done.2
  20.7 3.5 %collective-permute-start = (f32[24,512]{1,0:T(8,128)S(1)}, f32[24,512]{1,0:T(8,128)S(1)}, u32[]{:S(2)}, u32[]{:S(2)}) collective-permute-start(f32[24,512]{1,0:T(8,128)S(1)} %copy-done.2), channel_id=1, source_target_pairs={{0,1},{1,2},{2,3},{3,4},{4,5},{5,6},{6,7},{8,9},{9,10},{10,11},{11... | collective-permute-start | bytes 147464 | tf_op jit(solution)/shard_map/ppermute | solution.py:375
  24.2 0.0 copy-start.1
  24.2 3.4 %collective-permute-done.passed_ref = f32[24,512]{1,0:T(8,128)S(1)} collective-permute-done((f32[24,512]{1,0:T(8,128)S(1)}, f32[24,512]{1,0:T(8,128)S(1)}, u32[]{:S(2)}, u32[]{:S(2)}) %collective-permute-start) | collective-permute-done | bytes 49184 | tf_op jit(solution)/shard_map/ppermute | solution.py:375
  27.6 0.0 copy-done
  27.6 0.0 copy-done.1
  27.6 0.8 %spectra.1 = bf16[2,128,256]{2,1,0:T(8,128)(2,1)} custom-call(f32[24,512]{1,0:T(8,128)S(1)} %collective-permute-done.passed_ref, f32[128,512]{1,0:T(8,128)S(1)} %copy-done, f32[2,8,256]{2,1,0:T(8,128)S(1)} %bitcast.14), custom_call_target="tpu_custom_call" | custom-call | flops 524288 | bytes 1048576 | tf_op jit(solution)/shard_map/spectra/pallas_call | solution.py:376
  28.4 1.9 %all-to-all-done = bf16[16,8,640]{2,1,0:T(8,128)(2,1)S(1)} async-done(((bf16[16,8,640]{2,1,0:T(8,128)(2,1)}), bf16[16,8,640]{2,1,0:T(8,128)(2,1)S(1)}, u32[]{:S(2)}, u32[]{:S(2)}) %all-to-all-start) | async-done | bytes 163872 | tf_op jit(solution)/shard_map/all_to_all | solution.py:372
  30.3 0.2 spread.1
  30.5 13.2 %all_to_all.15.refs_1_ = bf16[32,40,128]{2,1,0:T(8,128)(2,1)S(1)} all-to-all(bf16[32,40,128]{2,1,0:T(8,128)(2,1)S(1)} %spread.1), channel_id=1, replica_groups={{20,31,10,21,0,11,22,1,12,23,2,13,24,3,14,25,4,15,26,5,16,27,6,17,28,7,..., dimensions={0} | all-to-all | bytes 655360 | tf_op jit(solution)/shard_map/all_to_all | solution.py:407
  43.7 0.6 %correlate.1 = bf16[4,64,512]{2,1,0:T(8,128)(2,1)S(1)} custom-call(s32[1]{0:T(128)} %bitcast.5.refs_0_, bf16[32,40,128]{2,1,0:T(8,128)(2,1)S(1)} %all_to_all.15.refs_1_), custom_call_target="tpu_custom_call" | custom-call | tf_op jit(solution)/shard_map/correlate/pallas_call | solution.py:413
  44.3 8.9 %all_to_all.16.packed_ref = bf16[4,64,512]{2,1,0:T(8,128)(2,1)S(1)} all-to-all(bf16[4,64,512]{2,1,0:T(8,128)(2,1)S(1)} %correlate.1), channel_id=1, replica_groups={{0,1,2,3},{4,5,6,7},{8,9,10,11},{12,13,14,15},{16,17,18,19},{20,21,22,2..., dimensions={0} | all-to-all | bytes 524288 | tf_op jit(solution)/shard_map/all_to_all | solution.py:422
  53.2 0.9 %unpack.1 = f32[1024,128]{1,0:T(8,128)} custom-call(bf16[4,64,512]{2,1,0:T(8,128)(2,1)S(1)} %all_to_all.16.packed_ref), custom_call_target="tpu_custom_call" | custom-call | tf_op jit(solution)/shard_map/unpack/pallas_call | solution.py:424
Async XLA Ops:
  3.5 24.1 %copy-start = (f32[128,512]{1,0:T(8,128)S(1)}, f32[128,512]{1,0:T(8,128)}, u32[]{:S(2)}) copy-start(f32[128,512]{1,0:T(8,128)} %get-tuple-element.11.own_ref) | copy-start | bytes 786436
  3.5 17.2 %copy-start.2 = (f32[24,512]{1,0:T(8,128)S(1)}, f32[24,512]{1,0:T(8,128)}, u32[]{:S(2)}) copy-start(f32[24,512]{1,0:T(8,128)} %get-tuple-element.10) | copy-start | bytes 147460
  3.5 26.8 %all-to-all-start = ((bf16[16,8,640]{2,1,0:T(8,128)(2,1)}), bf16[16,8,640]{2,1,0:T(8,128)(2,1)S(1)}, u32[]{:S(2)}, u32[]{:S(2)}) async-start(bf16[16,8,640]{2,1,0:T(8,128)(2,1)} %bitcast.16), calls=%async_computation | async-start | bytes 327680 | tf_op jit(solution)/shard_map/all_to_all | solution.py:372
  20.7 6.9 %collective-permute-start = (f32[24,512]{1,0:T(8,128)S(1)}, f32[24,512]{1,0:T(8,128)S(1)}, u32[]{:S(2)}, u32[]{:S(2)}) collective-permute-start(f32[24,512]{1,0:T(8,128)S(1)} %copy-done.2), channel_id=1, source_target_pairs={{0,1},{1,2},{2,3},{3,4},{4,5},{5,6},{6,7},{8,9},{9,10},{10,11},{11... | collective-permute-start | bytes 147464 | tf_op jit(solution)/shard_map/ppermute | solution.py:375
  24.2 3.4 %copy-start.1 = (f32[2,256,8]{1,2,0:T(8,128)S(1)}, f32[2,256,8]{1,2,0:T(8,128)}, u32[]{:S(2)}) copy-start(f32[2,256,8]{1,2,0:T(8,128)} %param.5) | copy-start | bytes 49156

commit v4 on v2

--- a/solution.py
+++ b/solution.py
@@ -295,7 +295,7 @@
     values = jnp.where(row_index <= col_index, both[:held], both[held:]) * (1.0 / frames_all)
     values = values.astype(jnp.bfloat16)
     for block in range(blocks):
-        packed_ref[block] = values[block * rows : (block + 1) * rows]
+        packed_ref[blocks - 1 - block] = values[block * rows : (block + 1) * rows]
 
 
 def unpack_kernel(packed_ref, lines_hbm, lines_ref, left):
@@ -305,7 +305,8 @@
     for first in range(0, count, 16):
         start = first * tiles * channels
         for channel in range(channels):
-            values = packed_ref[channel, first : first + 16, :].astype(jnp.float32)
+            values = packed_ref[channels - 1 - channel, first : first + 16, :]
+            values = values.astype(jnp.float32)
             for tile in range(tiles):
                 lines = pl.ds(start + tile * channels + channel, 16, stride=tiles * channels)
                 lines_ref[lines, :] = values[:, tile * LANES : (tile + 1) * LANES]
@@ -418,7 +419,7 @@
         compiler_params=PARAMS,
         name="correlate",
     )(square, every)
-    squares = [[0, 1, 2, 3], [4, 5, 6, 7]]
+    squares = [[3, 2, 1, 0], [7, 6, 5, 4]]
     packed = lax.all_to_all(packed, "tm", 0, 0, axis_index_groups=squares)
     tiles = inputs_all // LANES
     visibilities = pl.pallas_call(

time: 54.8 us -> 54.5 us (level)
  no operation moved by 1% of the time
where the time goes in v4:
time: 54.5 us; the launch traced here: 54.2 us
  blocking collectives  22 us (40%)
  starting transfers between devices  20.7 us (38%)
  waiting for transfers between devices  5.39 us (10%)
  Pallas kernels  5.36 us (10%)
  between operations  0.71 us (1%)
    all_to_all x1, starting transfers between devices, body(): mine = lax.all_to_all(parcels, 'far', 0, 0, axis_index_groups=column)  17.2 us
    all_to_all x1, blocking collectives, body(): lax.all_to_all(spread, ('near', 'tm'), 0, 0, axis_index_groups=plane)  13.2 us
    all_to_all x1, blocking collectives, body(): packed = lax.all_to_all(packed, 'tm', 0, 0, axis_index_groups=squares)  8.84 us
    ppermute x1, starting transfers between devices, body(): lax.ppermute(passed, 'tm', [(source, source + 1) for source in range(time...  3.49 us
    ppermute x1, waiting for transfers between devices, body(): lax.ppermute(passed, 'tm', [(source, source + 1) for source in range(time...  3.36 us
    pallas_call x1, Pallas kernels, body(): pl.pallas_call(own_part, out_shape=(jax.ShapeDtypeStruct((block, 2 * CH),...  2.86 us
    all_to_all x1, waiting for transfers between devices, body(): mine = lax.all_to_all(parcels, 'far', 0, 0, axis_index_groups=column)  2.02 us
  transfers between devices with their start and end apart: 2, of which 2 were waited for; matrix products, arithmetic and copies ran while one was open for 0% of the time, Pallas kernels for 1%

profile of v4, /device:TPU:6, one launch (start us, length us, event | category | flops | bytes accessed | tf_op | source)
XLA Modules:
  0.0 54.2 jit_solution(13744212987347018363)
XLA Ops:
  0.6 2.9 %own_part.1 = (f32[128,512]{1,0:T(8,128)}, f32[24,512]{1,0:T(8,128)}, bf16[128,640]{1,0:T(8,128)(2,1)}) custom-call(bf16[8,32768]{1,0:T(8,128)(2,1)} %refs_0_.1, f32[4,2048]{1,0:T(4,128)} %constant.25.clone.refs_1_, bf16[1024,512]{1,0:T(8,128)(2,1)} %constant.24.clone.refs_2_, f32[2,8,256]{2,1,0:T(8,128)} %bitcast.13), custom_call_target="tpu_custom_call" | custom-call | flops 335544320 | bytes 3145728 | tf_op jit(solution)/shard_map/own_part/pallas_call | solution.py:343
  3.5 0.0 copy-start
  3.5 0.0 copy-start.2
  3.5 17.2 %all-to-all-start = ((bf16[16,8,640]{2,1,0:T(8,128)(2,1)}), bf16[16,8,640]{2,1,0:T(8,128)(2,1)S(1)}, u32[]{:S(2)}, u32[]{:S(2)}) async-start(bf16[16,8,640]{2,1,0:T(8,128)(2,1)} %bitcast.16), calls=%async_computation | async-start | bytes 327680 | tf_op jit(solution)/shard_map/all_to_all | solution.py:373
  20.7 0.0 copy-done.2
  20.7 3.5 %collective-permute-start = (f32[24,512]{1,0:T(8,128)S(1)}, f32[24,512]{1,0:T(8,128)S(1)}, u32[]{:S(2)}, u32[]{:S(2)}) collective-permute-start(f32[24,512]{1,0:T(8,128)S(1)} %copy-done.2), channel_id=1, source_target_pairs={{0,1},{1,2},{2,3},{3,4},{4,5},{5,6},{6,7},{8,9},{9,10},{10,11},{11... | collective-permute-start | bytes 147464 | tf_op jit(solution)/shard_map/ppermute | solution.py:376
  24.2 0.0 copy-start.1
  24.2 3.4 %collective-permute-done.passed_ref = f32[24,512]{1,0:T(8,128)S(1)} collective-permute-done((f32[24,512]{1,0:T(8,128)S(1)}, f32[24,512]{1,0:T(8,128)S(1)}, u32[]{:S(2)}, u32[]{:S(2)}) %collective-permute-start) | collective-permute-done | bytes 49184 | tf_op jit(solution)/shard_map/ppermute | solution.py:376
  27.6 0.0 copy-done
  27.6 0.0 copy-done.1
  27.6 0.8 %spectra.1 = bf16[2,128,256]{2,1,0:T(8,128)(2,1)} custom-call(f32[24,512]{1,0:T(8,128)S(1)} %collective-permute-done.passed_ref, f32[128,512]{1,0:T(8,128)S(1)} %copy-done, f32[2,8,256]{2,1,0:T(8,128)S(1)} %bitcast.14), custom_call_target="tpu_custom_call" | custom-call | flops 524288 | bytes 1048576 | tf_op jit(solution)/shard_map/spectra/pallas_call | solution.py:377
  28.4 2.0 %all-to-all-done = bf16[16,8,640]{2,1,0:T(8,128)(2,1)S(1)} async-done(((bf16[16,8,640]{2,1,0:T(8,128)(2,1)}), bf16[16,8,640]{2,1,0:T(8,128)(2,1)S(1)}, u32[]{:S(2)}, u32[]{:S(2)}) %all-to-all-start) | async-done | bytes 163872 | tf_op jit(solution)/shard_map/all_to_all | solution.py:373
  30.4 0.2 spread.1
  30.6 13.2 %all_to_all.15.refs_1_ = bf16[32,40,128]{2,1,0:T(8,128)(2,1)S(1)} all-to-all(bf16[32,40,128]{2,1,0:T(8,128)(2,1)S(1)} %spread.1), channel_id=1, replica_groups={{20,31,10,21,0,11,22,1,12,23,2,13,24,3,14,25,4,15,26,5,16,27,6,17,28,7,..., dimensions={0} | all-to-all | bytes 655360 | tf_op jit(solution)/shard_map/all_to_all | solution.py:408
  43.8 0.6 %correlate.1 = bf16[4,64,512]{2,1,0:T(8,128)(2,1)S(1)} custom-call(s32[1]{0:T(128)} %bitcast.5.refs_0_, bf16[32,40,128]{2,1,0:T(8,128)(2,1)S(1)} %all_to_all.15.refs_1_), custom_call_target="tpu_custom_call" | custom-call | tf_op jit(solution)/shard_map/correlate/pallas_call | solution.py:414
  44.5 8.8 %all_to_all.16.packed_ref = bf16[4,64,512]{2,1,0:T(8,128)(2,1)S(1)} all-to-all(bf16[4,64,512]{2,1,0:T(8,128)(2,1)S(1)} %correlate.1), channel_id=1, replica_groups={{3,2,1,0},{7,6,5,4},{11,10,9,8},{15,14,13,12},{19,18,17,16},{23,22,21,2..., dimensions={0} | all-to-all | bytes 524288 | tf_op jit(solution)/shard_map/all_to_all | solution.py:423
  53.3 0.9 %unpack.1 = f32[1024,128]{1,0:T(8,128)} custom-call(bf16[4,64,512]{2,1,0:T(8,128)(2,1)S(1)} %all_to_all.16.packed_ref), custom_call_target="tpu_custom_call" | custom-call | tf_op jit(solution)/shard_map/unpack/pallas_call | solution.py:425
Async XLA Ops:
  3.5 24.1 %copy-start = (f32[128,512]{1,0:T(8,128)S(1)}, f32[128,512]{1,0:T(8,128)}, u32[]{:S(2)}) copy-start(f32[128,512]{1,0:T(8,128)} %get-tuple-element.11.own_ref) | copy-start | bytes 786436
  3.5 17.2 %copy-start.2 = (f32[24,512]{1,0:T(8,128)S(1)}, f32[24,512]{1,0:T(8,128)}, u32[]{:S(2)}) copy-start(f32[24,512]{1,0:T(8,128)} %get-tuple-element.10) | copy-start | bytes 147460
  3.5 26.9 %all-to-all-start = ((bf16[16,8,640]{2,1,0:T(8,128)(2,1)}), bf16[16,8,640]{2,1,0:T(8,128)(2,1)S(1)}, u32[]{:S(2)}, u32[]{:S(2)}) async-start(bf16[16,8,640]{2,1,0:T(8,128)(2,1)} %bitcast.16), calls=%async_computation | async-start | bytes 327680 | tf_op jit(solution)/shard_map/all_to_all | solution.py:373
  20.7 6.9 %collective-permute-start = (f32[24,512]{1,0:T(8,128)S(1)}, f32[24,512]{1,0:T(8,128)S(1)}, u32[]{:S(2)}, u32[]{:S(2)}) collective-permute-start(f32[24,512]{1,0:T(8,128)S(1)} %copy-done.2), channel_id=1, source_target_pairs={{0,1},{1,2},{2,3},{3,4},{4,5},{5,6},{6,7},{8,9},{9,10},{10,11},{11... | collective-permute-start | bytes 147464 | tf_op jit(solution)/shard_map/ppermute | solution.py:376
  24.2 3.4 %copy-start.1 = (f32[2,256,8]{1,2,0:T(8,128)S(1)}, f32[2,256,8]{1,2,0:T(8,128)}, u32[]{:S(2)}) copy-start(f32[2,256,8]{1,2,0:T(8,128)} %param.5) | copy-start | bytes 49156

commit v5 on v4

--- a/solution.py
+++ b/solution.py
@@ -225,6 +225,10 @@
     return time % 4
 
 
+def place_in_square(member, square):
+    return member ^ (3 - 2 * square)
+
+
 def place_in_plane(near, time, times):
     count = NEAR * times
     middle = NEAR // 2 * times + times // 2
@@ -295,17 +299,18 @@
     values = jnp.where(row_index <= col_index, both[:held], both[held:]) * (1.0 / frames_all)
     values = values.astype(jnp.bfloat16)
     for block in range(blocks):
-        packed_ref[blocks - 1 - block] = values[block * rows : (block + 1) * rows]
-
-
-def unpack_kernel(packed_ref, lines_hbm, lines_ref, left):
+        target = place_in_square(block, place_ref[0])
+        packed_ref[target] = values[block * rows : (block + 1) * rows]
+
+
+def unpack_kernel(place_ref, packed_ref, lines_hbm, lines_ref, left):
     channels, count, width = packed_ref.shape
     tiles = width // LANES
     stores = []
     for first in range(0, count, 16):
         start = first * tiles * channels
         for channel in range(channels):
-            values = packed_ref[channels - 1 - channel, first : first + 16, :]
+            values = packed_ref[place_in_square(channel, place_ref[0]), first : first + 16, :]
             values = values.astype(jnp.float32)
             for tile in range(tiles):
                 lines = pl.ds(start + tile * channels + channel, 16, stride=tiles * channels)
@@ -419,13 +424,16 @@
         compiler_params=PARAMS,
         name="correlate",
     )(square, every)
-    squares = [[3, 2, 1, 0], [7, 6, 5, 4]]
+    squares = [
+        [4 * side + place_in_square(member, side) for member in range(per_group)]
+        for side in range(2)
+    ]
     packed = lax.all_to_all(packed, "tm", 0, 0, axis_index_groups=squares)
     tiles = inputs_all // LANES
     visibilities = pl.pallas_call(
         unpack_kernel,
         out_shape=jax.ShapeDtypeStruct((rows * tiles * per_group, LANES), jnp.float32),
-        in_specs=[VMEM],
+        in_specs=[SMEM, VMEM],
         out_specs=ANY,
         scratch_shapes=[
             pltpu.VMEM(((rows + 1) * tiles * per_group, LANES), jnp.float32),
@@ -433,7 +441,7 @@
         ],
         compiler_params=PARAMS,
         name="unpack",
-    )(packed)
+    )(square, packed)
     visibilities = visibilities.reshape(rows, tiles, per_group, LANES).transpose(0, 2, 1, 3)
     visibilities = visibilities.reshape(rows, per_group, inputs_all)
     return (spectra, visibilities)

time: 54.5 us -> 54.7 us (level); the launches traced: 54.2 us -> 53.8 us
  no operation moved by 1% of the time
where the time goes in v5:
time: 54.7 us; the launch traced here: 53.8 us
  blocking collectives  21.7 us (40%)
  starting transfers between devices  20.7 us (38%)
  waiting for transfers between devices  5.39 us (10%)
  Pallas kernels  5.36 us (10%)
  between operations  0.71 us (1%)
    all_to_all x1, starting transfers between devices, body(): mine = lax.all_to_all(parcels, 'far', 0, 0, axis_index_groups=column)  17.2 us
    all_to_all x1, blocking collectives, body(): lax.all_to_all(spread, ('near', 'tm'), 0, 0, axis_index_groups=plane)  13.2 us
    all_to_all x1, blocking collectives, body(): packed = lax.all_to_all(packed, 'tm', 0, 0, axis_index_groups=squares)  8.49 us
    ppermute x1, starting transfers between devices, body(): lax.ppermute(passed, 'tm', [(source, source + 1) for source in range(time...  3.49 us
    ppermute x1, waiting for transfers between devices, body(): lax.ppermute(passed, 'tm', [(source, source + 1) for source in range(time...  3.36 us
    pallas_call x1, Pallas kernels, body(): pl.pallas_call(own_part, out_shape=(jax.ShapeDtypeStruct((block, 2 * CH),...  2.86 us
    all_to_all x1, waiting for transfers between devices, body(): mine = lax.all_to_all(parcels, 'far', 0, 0, axis_index_groups=column)  2.02 us
  transfers between devices with their start and end apart: 2, of which 2 were waited for; matrix products, arithmetic and copies ran while one was open for 0% of the time, Pallas kernels for 1%

profile of v5, /device:TPU:6, one launch (start us, length us, event | category | flops | bytes accessed | tf_op | source)
XLA Modules:
  0.0 53.8 jit_solution(13602481160114719020)
XLA Ops:
  0.6 2.9 %own_part.1 = (f32[128,512]{1,0:T(8,128)}, f32[24,512]{1,0:T(8,128)}, bf16[128,640]{1,0:T(8,128)(2,1)}) custom-call(bf16[8,32768]{1,0:T(8,128)(2,1)} %refs_0_.1, f32[4,2048]{1,0:T(4,128)} %constant.25.clone.refs_1_, bf16[1024,512]{1,0:T(8,128)(2,1)} %constant.24.clone.refs_2_, f32[2,8,256]{2,1,0:T(8,128)} %bitcast.13), custom_call_target="tpu_custom_call" | custom-call | flops 335544320 | bytes 3145728 | tf_op jit(solution)/shard_map/own_part/pallas_call | solution.py:348
  3.5 0.0 copy-start
  3.5 0.0 copy-start.2
  3.5 17.2 %all-to-all-start = ((bf16[16,8,640]{2,1,0:T(8,128)(2,1)}), bf16[16,8,640]{2,1,0:T(8,128)(2,1)S(1)}, u32[]{:S(2)}, u32[]{:S(2)}) async-start(bf16[16,8,640]{2,1,0:T(8,128)(2,1)} %bitcast.16), calls=%async_computation | async-start | bytes 327680 | tf_op jit(solution)/shard_map/all_to_all | solution.py:378
  20.7 0.0 copy-done.2
  20.7 3.5 %collective-permute-start = (f32[24,512]{1,0:T(8,128)S(1)}, f32[24,512]{1,0:T(8,128)S(1)}, u32[]{:S(2)}, u32[]{:S(2)}) collective-permute-start(f32[24,512]{1,0:T(8,128)S(1)} %copy-done.2), channel_id=1, source_target_pairs={{0,1},{1,2},{2,3},{3,4},{4,5},{5,6},{6,7},{8,9},{9,10},{10,11},{11... | collective-permute-start | bytes 147464 | tf_op jit(solution)/shard_map/ppermute | solution.py:381
  24.2 0.0 copy-start.1
  24.2 3.4 %collective-permute-done.passed_ref = f32[24,512]{1,0:T(8,128)S(1)} collective-permute-done((f32[24,512]{1,0:T(8,128)S(1)}, f32[24,512]{1,0:T(8,128)S(1)}, u32[]{:S(2)}, u32[]{:S(2)}) %collective-permute-start) | collective-permute-done | bytes 49184 | tf_op jit(solution)/shard_map/ppermute | solution.py:381
  27.6 0.0 copy-done
  27.6 0.0 copy-done.1
  27.6 0.8 %spectra.1 = bf16[2,128,256]{2,1,0:T(8,128)(2,1)} custom-call(f32[24,512]{1,0:T(8,128)S(1)} %collective-permute-done.passed_ref, f32[128,512]{1,0:T(8,128)S(1)} %copy-done, f32[2,8,256]{2,1,0:T(8,128)S(1)} %bitcast.14), custom_call_target="tpu_custom_call" | custom-call | flops 524288 | bytes 1048576 | tf_op jit(solution)/shard_map/spectra/pallas_call | solution.py:382
  28.4 2.0 %all-to-all-done = bf16[16,8,640]{2,1,0:T(8,128)(2,1)S(1)} async-done(((bf16[16,8,640]{2,1,0:T(8,128)(2,1)}), bf16[16,8,640]{2,1,0:T(8,128)(2,1)S(1)}, u32[]{:S(2)}, u32[]{:S(2)}) %all-to-all-start) | async-done | bytes 163872 | tf_op jit(solution)/shard_map/all_to_all | solution.py:378
  30.4 0.2 spread.1
  30.6 13.2 %all_to_all.15.refs_1_ = bf16[32,40,128]{2,1,0:T(8,128)(2,1)S(1)} all-to-all(bf16[32,40,128]{2,1,0:T(8,128)(2,1)S(1)} %spread.1), channel_id=1, replica_groups={{20,31,10,21,0,11,22,1,12,23,2,13,24,3,14,25,4,15,26,5,16,27,6,17,28,7,..., dimensions={0} | all-to-all | bytes 655360 | tf_op jit(solution)/shard_map/all_to_all | solution.py:413
  43.8 0.6 %correlate.1 = bf16[4,64,512]{2,1,0:T(8,128)(2,1)S(1)} custom-call(s32[1]{0:T(128)} %bitcast.5.refs_0_.place_ref, bf16[32,40,128]{2,1,0:T(8,128)(2,1)S(1)} %all_to_all.15.refs_1_), custom_call_target="tpu_custom_call" | custom-call | tf_op jit(solution)/shard_map/correlate/pallas_call | solution.py:419
  44.5 8.5 %all_to_all.16.packed_ref = bf16[4,64,512]{2,1,0:T(8,128)(2,1)S(1)} all-to-all(bf16[4,64,512]{2,1,0:T(8,128)(2,1)S(1)} %correlate.1), channel_id=1, replica_groups={{3,2,1,0},{5,4,7,6},{11,10,9,8},{13,12,15,14},{19,18,17,16},{21,20,23,2..., dimensions={0} | all-to-all | bytes 524288 | tf_op jit(solution)/shard_map/all_to_all | solution.py:431
  52.9 0.9 %unpack.1 = f32[1024,128]{1,0:T(8,128)} custom-call(s32[1]{0:T(128)} %bitcast.5.refs_0_.place_ref, bf16[4,64,512]{2,1,0:T(8,128)(2,1)S(1)} %all_to_all.16.packed_ref), custom_call_target="tpu_custom_call" | custom-call | tf_op jit(solution)/shard_map/unpack/pallas_call | solution.py:433
Async XLA Ops:
  3.5 24.1 %copy-start = (f32[128,512]{1,0:T(8,128)S(1)}, f32[128,512]{1,0:T(8,128)}, u32[]{:S(2)}) copy-start(f32[128,512]{1,0:T(8,128)} %get-tuple-element.11.own_ref) | copy-start | bytes 786436
  3.5 17.2 %copy-start.2 = (f32[24,512]{1,0:T(8,128)S(1)}, f32[24,512]{1,0:T(8,128)}, u32[]{:S(2)}) copy-start(f32[24,512]{1,0:T(8,128)} %get-tuple-element.10) | copy-start | bytes 147460
  3.5 26.9 %all-to-all-start = ((bf16[16,8,640]{2,1,0:T(8,128)(2,1)}), bf16[16,8,640]{2,1,0:T(8,128)(2,1)S(1)}, u32[]{:S(2)}, u32[]{:S(2)}) async-start(bf16[16,8,640]{2,1,0:T(8,128)(2,1)} %bitcast.16), calls=%async_computation | async-start | bytes 327680 | tf_op jit(solution)/shard_map/all_to_all | solution.py:378
  20.7 6.9 %collective-permute-start = (f32[24,512]{1,0:T(8,128)S(1)}, f32[24,512]{1,0:T(8,128)S(1)}, u32[]{:S(2)}, u32[]{:S(2)}) collective-permute-start(f32[24,512]{1,0:T(8,128)S(1)} %copy-done.2), channel_id=1, source_target_pairs={{0,1},{1,2},{2,3},{3,4},{4,5},{5,6},{6,7},{8,9},{9,10},{10,11},{11... | collective-permute-start | bytes 147464 | tf_op jit(solution)/shard_map/ppermute | solution.py:381
  24.2 3.4 %copy-start.1 = (f32[2,256,8]{1,2,0:T(8,128)S(1)}, f32[2,256,8]{1,2,0:T(8,128)}, u32[]{:S(2)}) copy-start(f32[2,256,8]{1,2,0:T(8,128)} %param.5) | copy-start | bytes 49156

commit v6 on v4

--- a/solution.py
+++ b/solution.py
@@ -117,9 +117,9 @@
     samples_in = fetch(samples_hbm, samples_ref)
     window_in = fetch(window_hbm, window_ref)
     table_in = []
-    for block in blocks[: len(blocks) // 2]:
-        rows = pl.ds(block * STEP, STEP)
-        table_in.append(fetch(twiddle_hbm.at[rows, :], twiddle_ref.at[rows, :]))
+    for block in range(0, len(blocks) // 2, 2):
+        rows = pl.ds(block * STEP, 2 * STEP)
+        table_in += [fetch(twiddle_hbm.at[rows, :], twiddle_ref.at[rows, :]), None]
     gains_in = fetch(gains_hbm, gains_ref)
     samples_in.wait()
     window_in.wait()
@@ -130,7 +130,8 @@
             tapped_block(samples_ref, window_ref, sent, half + block)
             for half in (0, len(table_in))
         ]
-        table.wait()
+        if table is not None:
+            table.wait()
         product = jnp.dot(
             jnp.concatenate(tapped, axis=0),
             twiddle_ref[block * STEP : (block + 1) * STEP, :],
@@ -183,13 +184,15 @@
             parcels_ref[rows, columns] = jnp.concatenate(
                 [blocks[target] for target in listed[index : index + 2]], axis=0
             ).astype(jnp.bfloat16)
-        lanes = pl.ds(place * LANES, LANES)
-        stores.append(
-            pltpu.make_async_copy(
-                parcels_ref.at[:, lanes], parcels_hbm.at[:, lanes], left.at[len(stores)]
+        if place in (2, len(slots) - 1):
+            first = 0 if place == 2 else 3
+            lanes = pl.ds(first * LANES, (place + 1 - first) * LANES)
+            stores.append(
+                pltpu.make_async_copy(
+                    parcels_ref.at[:, lanes], parcels_hbm.at[:, lanes], left.at[len(stores)]
+                )
             )
-        )
-        stores[-1].start()
+            stores[-1].start()
     for store in stores:
         store.wait()
 
@@ -302,15 +305,15 @@
     channels, count, width = packed_ref.shape
     tiles = width // LANES
     stores = []
-    for first in range(0, count, 16):
+    for first in range(0, count, 32):
         start = first * tiles * channels
         for channel in range(channels):
-            values = packed_ref[channels - 1 - channel, first : first + 16, :]
+            values = packed_ref[channels - 1 - channel, first : first + 32, :]
             values = values.astype(jnp.float32)
             for tile in range(tiles):
-                lines = pl.ds(start + tile * channels + channel, 16, stride=tiles * channels)
+                lines = pl.ds(start + tile * channels + channel, 32, stride=tiles * channels)
                 lines_ref[lines, :] = values[:, tile * LANES : (tile + 1) * LANES]
-        block = pl.ds(start, 16 * tiles * channels)
+        block = pl.ds(start, 32 * tiles * channels)
         stores.append(
             pltpu.make_async_copy(lines_ref.at[block, :], lines_hbm.at[block, :], left.at[len(stores)])
         )
@@ -356,8 +359,8 @@
             pltpu.VMEM(gains.shape, jnp.float32),
             pltpu.VMEM((sent * inputs_here, 2 * CH), jnp.float32),
             pltpu.VMEM((far * inputs_here, sent * 2 * CH // far), jnp.bfloat16),
-            pltpu.SemaphoreType.DMA((3 + NFFT // (2 * STEP),)),
-            pltpu.SemaphoreType.DMA((2 + sent // 4,)),
+            pltpu.SemaphoreType.DMA((3 + NFFT // (4 * STEP),)),
+            pltpu.SemaphoreType.DMA((4,)),
         ],
         compiler_params=pltpu.CompilerParams(vmem_limit_bytes=OWN_PART_VMEM),
         cost_estimate=pl.CostEstimate(
@@ -429,7 +432,7 @@
         out_specs=ANY,
         scratch_shapes=[
             pltpu.VMEM(((rows + 1) * tiles * per_group, LANES), jnp.float32),
-            pltpu.SemaphoreType.DMA((rows // 16,)),
+            pltpu.SemaphoreType.DMA((rows // 32,)),
         ],
         compiler_params=PARAMS,
         name="unpack",

time: 54.5 us -> 54.5 us (level)
  no operation moved by 1% of the time
where the time goes in v6:
time: 54.5 us; the launch traced here: 54.2 us
  blocking collectives  22 us (40%)
  starting transfers between devices  20.7 us (38%)
  Pallas kernels  5.4 us (10%)
  waiting for transfers between devices  5.39 us (10%)
  between operations  0.71 us (1%)
    all_to_all x1, starting transfers between devices, body(): mine = lax.all_to_all(parcels, 'far', 0, 0, axis_index_groups=column)  17.2 us
    all_to_all x1, blocking collectives, body(): lax.all_to_all(spread, ('near', 'tm'), 0, 0, axis_index_groups=plane)  13.2 us
    all_to_all x1, blocking collectives, body(): packed = lax.all_to_all(packed, 'tm', 0, 0, axis_index_groups=squares)  8.85 us
    ppermute x1, starting transfers between devices, body(): lax.ppermute(passed, 'tm', [(source, source + 1) for source in range(time...  3.48 us
    ppermute x1, waiting for transfers between devices, body(): lax.ppermute(passed, 'tm', [(source, source + 1) for source in range(time...  3.37 us
    pallas_call x1, Pallas kernels, body(): pl.pallas_call(own_part, out_shape=(jax.ShapeDtypeStruct((block, 2 * CH),...  2.82 us
    all_to_all x1, waiting for transfers between devices, body(): mine = lax.all_to_all(parcels, 'far', 0, 0, axis_index_groups=column)  2.02 us
  transfers between devices with their start and end apart: 2, of which 2 were waited for; matrix products, arithmetic and copies ran while one was open for 0% of the time, Pallas kernels for 1%

profile of v6, /device:TPU:6, one launch (start us, length us, event | category | flops | bytes accessed | tf_op | source)
XLA Modules:
  0.0 54.2 jit_solution(660928499226767464)
XLA Ops:
  0.6 2.8 %own_part.1 = (f32[128,512]{1,0:T(8,128)}, f32[24,512]{1,0:T(8,128)}, bf16[128,640]{1,0:T(8,128)(2,1)}) custom-call(bf16[8,32768]{1,0:T(8,128)(2,1)} %refs_0_.1, f32[4,2048]{1,0:T(4,128)} %constant.25.clone.refs_1_, bf16[1024,512]{1,0:T(8,128)(2,1)} %constant.24.clone.refs_2_, f32[2,8,256]{2,1,0:T(8,128)} %bitcast.13), custom_call_target="tpu_custom_call" | custom-call | flops 335544320 | bytes 3145728 | tf_op jit(solution)/shard_map/own_part/pallas_call | solution.py:346
  3.5 0.0 copy-start
  3.5 0.0 copy-start.2
  3.5 17.2 %all-to-all-start = ((bf16[16,8,640]{2,1,0:T(8,128)(2,1)}), bf16[16,8,640]{2,1,0:T(8,128)(2,1)S(1)}, u32[]{:S(2)}, u32[]{:S(2)}) async-start(bf16[16,8,640]{2,1,0:T(8,128)(2,1)} %bitcast.16), calls=%async_computation | async-start | bytes 327680 | tf_op jit(solution)/shard_map/all_to_all | solution.py:376
  20.7 0.0 copy-done.2
  20.7 3.5 %collective-permute-start = (f32[24,512]{1,0:T(8,128)S(1)}, f32[24,512]{1,0:T(8,128)S(1)}, u32[]{:S(2)}, u32[]{:S(2)}) collective-permute-start(f32[24,512]{1,0:T(8,128)S(1)} %copy-done.2), channel_id=1, source_target_pairs={{0,1},{1,2},{2,3},{3,4},{4,5},{5,6},{6,7},{8,9},{9,10},{10,11},{11... | collective-permute-start | bytes 147464 | tf_op jit(solution)/shard_map/ppermute | solution.py:379
  24.2 0.0 copy-start.1
  24.2 3.4 %collective-permute-done.passed_ref = f32[24,512]{1,0:T(8,128)S(1)} collective-permute-done((f32[24,512]{1,0:T(8,128)S(1)}, f32[24,512]{1,0:T(8,128)S(1)}, u32[]{:S(2)}, u32[]{:S(2)}) %collective-permute-start) | collective-permute-done | bytes 49184 | tf_op jit(solution)/shard_map/ppermute | solution.py:379
  27.6 0.0 copy-done
  27.6 0.0 copy-done.1
  27.6 0.8 %spectra.1 = bf16[2,128,256]{2,1,0:T(8,128)(2,1)} custom-call(f32[24,512]{1,0:T(8,128)S(1)} %collective-permute-done.passed_ref, f32[128,512]{1,0:T(8,128)S(1)} %copy-done, f32[2,8,256]{2,1,0:T(8,128)S(1)} %bitcast.14), custom_call_target="tpu_custom_call" | custom-call | flops 524288 | bytes 1048576 | tf_op jit(solution)/shard_map/spectra/pallas_call | solution.py:380
  28.4 2.0 %all-to-all-done = bf16[16,8,640]{2,1,0:T(8,128)(2,1)S(1)} async-done(((bf16[16,8,640]{2,1,0:T(8,128)(2,1)}), bf16[16,8,640]{2,1,0:T(8,128)(2,1)S(1)}, u32[]{:S(2)}, u32[]{:S(2)}) %all-to-all-start) | async-done | bytes 163872 | tf_op jit(solution)/shard_map/all_to_all | solution.py:376
  30.4 0.2 spread.1
  30.6 13.2 %all_to_all.15.refs_1_ = bf16[32,40,128]{2,1,0:T(8,128)(2,1)S(1)} all-to-all(bf16[32,40,128]{2,1,0:T(8,128)(2,1)S(1)} %spread.1), channel_id=1, replica_groups={{20,31,10,21,0,11,22,1,12,23,2,13,24,3,14,25,4,15,26,5,16,27,6,17,28,7,..., dimensions={0} | all-to-all | bytes 655360 | tf_op jit(solution)/shard_map/all_to_all | solution.py:411
  43.8 0.6 %correlate.1 = bf16[4,64,512]{2,1,0:T(8,128)(2,1)S(1)} custom-call(s32[1]{0:T(128)} %bitcast.5.refs_0_, bf16[32,40,128]{2,1,0:T(8,128)(2,1)S(1)} %all_to_all.15.refs_1_), custom_call_target="tpu_custom_call" | custom-call | tf_op jit(solution)/shard_map/correlate/pallas_call | solution.py:417
  44.4 8.9 %all_to_all.16.packed_ref = bf16[4,64,512]{2,1,0:T(8,128)(2,1)S(1)} all-to-all(bf16[4,64,512]{2,1,0:T(8,128)(2,1)S(1)} %correlate.1), channel_id=1, replica_groups={{3,2,1,0},{7,6,5,4},{11,10,9,8},{15,14,13,12},{19,18,17,16},{23,22,21,2..., dimensions={0} | all-to-all | bytes 524288 | tf_op jit(solution)/shard_map/all_to_all | solution.py:426
  53.3 0.9 %unpack.1 = f32[1024,128]{1,0:T(8,128)} custom-call(bf16[4,64,512]{2,1,0:T(8,128)(2,1)S(1)} %all_to_all.16.packed_ref), custom_call_target="tpu_custom_call" | custom-call | tf_op jit(solution)/shard_map/unpack/pallas_call | solution.py:428
Async XLA Ops:
  3.5 24.1 %copy-start = (f32[128,512]{1,0:T(8,128)S(1)}, f32[128,512]{1,0:T(8,128)}, u32[]{:S(2)}) copy-start(f32[128,512]{1,0:T(8,128)} %get-tuple-element.11.own_ref) | copy-start | bytes 786436
  3.5 17.2 %copy-start.2 = (f32[24,512]{1,0:T(8,128)S(1)}, f32[24,512]{1,0:T(8,128)}, u32[]{:S(2)}) copy-start(f32[24,512]{1,0:T(8,128)} %get-tuple-element.10) | copy-start | bytes 147460
  3.5 26.9 %all-to-all-start = ((bf16[16,8,640]{2,1,0:T(8,128)(2,1)}), bf16[16,8,640]{2,1,0:T(8,128)(2,1)S(1)}, u32[]{:S(2)}, u32[]{:S(2)}) async-start(bf16[16,8,640]{2,1,0:T(8,128)(2,1)} %bitcast.16), calls=%async_computation | async-start | bytes 327680 | tf_op jit(solution)/shard_map/all_to_all | solution.py:376
  20.7 6.9 %collective-permute-start = (f32[24,512]{1,0:T(8,128)S(1)}, f32[24,512]{1,0:T(8,128)S(1)}, u32[]{:S(2)}, u32[]{:S(2)}) collective-permute-start(f32[24,512]{1,0:T(8,128)S(1)} %copy-done.2), channel_id=1, source_target_pairs={{0,1},{1,2},{2,3},{3,4},{4,5},{5,6},{6,7},{8,9},{9,10},{10,11},{11... | collective-permute-start | bytes 147464 | tf_op jit(solution)/shard_map/ppermute | solution.py:379
  24.2 3.4 %copy-start.1 = (f32[2,256,8]{1,2,0:T(8,128)S(1)}, f32[2,256,8]{1,2,0:T(8,128)}, u32[]{:S(2)}) copy-start(f32[2,256,8]{1,2,0:T(8,128)} %param.5) | copy-start | bytes 49156
